TPU v7x, 32 devices: a whole 2x2x4 slice. The times are simulated.
32 devices in a mesh: seq: 8 (over z, x), head: 4 (over y, core).
Axes of the slice: x: 2, y: 2, z: 4, core: 2. Of those that a mesh axis runs over, the one named last changes fastest.
Arguments:
- queries: bfloat16 [1024, 8192], P('seq', 'head'), may hold values from -6 to 6
- memory_keys: bfloat16 [1024, 8192], P('seq', 'head'), may hold values from -6 to 6
- memory_values: bfloat16 [1024, 8192], P('seq', 'head'), may hold values from -6 to 6
- log_decay: float32 [1024, 64], P('seq', 'head'), may hold values from -3 to 0, as said below
- hidden_in: int32 [1024, 6144], P('seq', 'head'), may hold values from -127 to 127
- out_weight: bfloat16 [8192, 6144], P('head'), may hold values from -1 to 1, as said below
- routes: int32 [1024, 2], P('seq'), may hold values from 0 to 3, all different within a row; in each aligned block of 128 rows (0 to 127, 128 to 255, ...) at most 80 rows name the same one
- route_weight: float32 [1024, 2], P('seq'), may hold values from 0.25 to 1
- gate_weight: bfloat16 [6144, 36864], P(None, ('seq', 'head')), may hold values from -1 to 1, as said below
- up_weight: bfloat16 [6144, 36864], P(None, ('seq', 'head')), may hold values from -1 to 1, as said below
- down_weight: bfloat16 [36864, 6144], P(('seq', 'head')), may hold values from -1 to 1, as said below
- scales: float32 [14], replicated, may hold values from 0.5 to 2
Outputs:
- layer_out: bfloat16 [1024, 6144], P('seq', 'head')
Inputs may be any that keep to these rules, and one draw needn't show every extreme that they name: `routes`: each row names two different experts; among the rows of one device no expert is named by more than 80 rows. `log_decay`: every entry is negative. `out_weight`: every entry is -1, 0 or 1. `gate_weight`: every entry is -1, 0 or 1. `up_weight`: every entry is -1, 0 or 1. `down_weight`: every entry is -1, 0 or 1.
All inputs are finite; a program needn't handle non-finite values.
Results may differ from a plain program's by a relative error of at most 0.02.
Values may be sent and summed in bfloat16 or wider, within the bound.
A program may use at most 128 MiB of HBM per device.

v0:
```python
import jax
import jax.numpy as jnp
from jax import lax
from jax.sharding import PartitionSpec as P

D = 6144
FF = 9216
HEADS = 64
HEAD_DIM = 128
EXPERTS = 4
CAP = 80


def prefix(value, axis, combine, identity):
    length, mine = (lax.axis_size(axis), lax.axis_index(axis))
    everything = jax.tree.map(
        lambda part, kind: lax.all_gather(part.astype(kind), axis),
        value,
        (jnp.bfloat16, jnp.bfloat16),
    )
    start = jax.tree.map(
        lambda part, zero: jnp.broadcast_to(jnp.asarray(zero, part.dtype), part.shape),
        value,
        identity,
    )

    def hop(k, before):
        reached = k < mine
        new = combine(
            before, jax.tree.map(lambda part, own: part[k].astype(own.dtype), everything, value)
        )
        return jax.tree.map(lambda a, b: jnp.where(reached, a, b), new, before)

    return lax.fori_loop(0, length, hop, start)


def pack_rows(source, table, group):
    padded = jnp.concatenate([source, jnp.zeros((1, source.shape[1]), source.dtype)], axis=0)
    picked = padded[table].reshape(EXPERTS, CAP, source.shape[1])
    return jnp.repeat(picked, group, axis=0)


def route_rows(returned, group, routes, places, route_weight):
    width = returned.shape[2]
    summed = jnp.sum(returned.reshape(EXPERTS, group, CAP, width), axis=1, dtype=jnp.float32)
    chosen = jnp.take_along_axis(places, routes, axis=1)
    picked = summed.reshape(EXPERTS * CAP, width)[routes * CAP + chosen]
    return jnp.sum(route_weight[:, :, None] * picked, axis=1)


def combine_states(earlier, later):
    return (earlier[0] * later[0], later[0][:, None, None] * earlier[1] + later[1])


def local(
    queries,
    memory_keys,
    memory_values,
    log_decay,
    hidden_in,
    out_weight,
    routes,
    route_weight,
    gate_weight,
    up_weight,
    down_weight,
    scales,
):
    tokens = queries.shape[0]
    heads = log_decay.shape[1]
    sequence_count = lax.axis_size("seq")
    group = sequence_count // EXPERTS
    token_position = lax.axis_index("seq")
    owner = token_position // group
    query_rows = queries.reshape(tokens, heads, HEAD_DIM)
    key_rows = memory_keys.reshape(tokens, heads, HEAD_DIM)
    value_rows = memory_values.reshape(tokens, heads, HEAD_DIM)
    cumulative = jnp.cumsum(log_decay, axis=0)
    total = cumulative[tokens - 1]
    scores = jnp.einsum("thd,shd->hts", query_rows, key_rows, preferred_element_type=jnp.float32)
    spread = cumulative.T[:, :, None] - cumulative.T[:, None, :]
    causal = lax.broadcasted_iota(jnp.int32, (tokens, tokens), 0) >= lax.broadcasted_iota(
        jnp.int32, (tokens, tokens), 1
    )
    weights = jnp.where(causal[None], scores * jnp.exp(jnp.minimum(spread, 0.0)), 0.0).astype(
        jnp.bfloat16
    )
    inside = jnp.einsum("hts,shd->thd", weights, value_rows, preferred_element_type=jnp.float32)
    decayed = (
        key_rows.astype(jnp.float32) * jnp.exp(total[None, :] - cumulative)[:, :, None]
    ).astype(jnp.bfloat16)
    state = jnp.einsum("shd,she->hde", decayed, value_rows, preferred_element_type=jnp.float32)
    identity = (jnp.ones_like(total), jnp.zeros_like(state))
    carried = prefix((jnp.exp(total), state), "seq", combine_states, identity)[1]
    lifted = query_rows.astype(jnp.float32) * jnp.exp(cumulative)[:, :, None]
    across = jnp.einsum("thd,hde->the", lifted, carried, precision=lax.Precision.HIGHEST)
    mixer_output = inside + across
    heads_out = (
        mixer_output
        * lax.rsqrt(jnp.mean(mixer_output * mixer_output, axis=2, keepdims=True) + 1e-06)
    ).astype(jnp.bfloat16)
    mapped_vectors = jnp.dot(
        heads_out.reshape(tokens, heads * HEAD_DIM), out_weight, preferred_element_type=jnp.float32
    )
    attention = lax.psum_scatter(
        mapped_vectors.astype(jnp.bfloat16), "head", scatter_dimension=1, tiled=True
    ).astype(jnp.float32) * (scales[1] * 0.5 * (HEADS * HEAD_DIM) ** (-0.5))
    resid = scales[0] / 64.0 * hidden_in.astype(jnp.float32) + attention
    squares = lax.psum(jnp.sum(resid * resid, axis=1), "head")
    normed = (resid * lax.rsqrt(squares[:, None] / D + 1e-05)).astype(jnp.bfloat16)
    expert_ids = lax.broadcasted_iota(jnp.int32, (tokens, EXPERTS), 1)
    hits = jnp.logical_or(routes[:, 0:1] == expert_ids, routes[:, 1:2] == expert_ids).astype(
        jnp.int32
    )
    places = jnp.cumsum(hits, axis=0, dtype=jnp.int32) - hits
    target = jnp.where(hits > 0, expert_ids * CAP + places, EXPERTS * CAP).reshape(-1)
    sources = lax.broadcasted_iota(jnp.int32, (tokens, EXPERTS), 0).reshape(-1)
    table = jnp.full((EXPERTS * CAP,), tokens, jnp.int32).at[target].set(sources, mode="drop")
    gate_scale = scales[2 + owner] * D ** (-0.5)
    up_scale = scales[2 + EXPERTS + owner] * D ** (-0.5)
    down_scale = scales[2 + 2 * EXPERTS + owner] * FF ** (-0.5)
    received = lax.all_to_all(
        pack_rows(normed, table, group), "seq", split_axis=0, concat_axis=0, tiled=True
    )
    count = received.shape[1]
    piece = lax.all_gather(received, "head", axis=2, tiled=True)
    flat_rows = piece.reshape(sequence_count * count, piece.shape[2])
    gate = jnp.dot(flat_rows, gate_weight, preferred_element_type=jnp.float32)
    up = jnp.dot(flat_rows, up_weight, preferred_element_type=jnp.float32)
    act = (jax.nn.silu(gate * gate_scale) * (up * up_scale)).astype(jnp.bfloat16)
    part = (jnp.dot(act, down_weight, preferred_element_type=jnp.float32) * down_scale).astype(
        jnp.bfloat16
    )
    part = part.reshape(sequence_count, count, down_weight.shape[1])
    summed = lax.psum_scatter(
        lax.optimization_barrier(part).astype(jnp.float32).astype(jnp.bfloat16),
        "head",
        scatter_dimension=2,
        tiled=True,
    ).astype(jnp.float32)
    returned = lax.all_to_all(
        summed.astype(jnp.bfloat16), "seq", split_axis=0, concat_axis=0, tiled=True
    ).astype(summed.dtype)
    moe = route_rows(returned, group, routes, places, route_weight)
    return (resid + moe).astype(jnp.bfloat16)


def solution(mesh):
    placed = (
        P("seq", "head"),
        P("seq", "head"),
        P("seq", "head"),
        P("seq", "head"),
        P("seq", "head"),
        P("head", None),
        P("seq", None),
        P("seq", None),
        P(None, ("seq", "head")),
        P(None, ("seq", "head")),
        P(("seq", "head"), None),
        P(),
    )
    return jax.shard_map(
        local, mesh=mesh, in_specs=placed, out_specs=P("seq", "head"), check_vma=False
    )
```

profile of v0, /device:TPU:0, one launch (start us, length us, event | category | flops | bytes accessed | tf_op | source)
XLA Modules:
  0.0 436.0 jit_solution(16462556187351352257)
XLA Ops:
  9.0 2.1 convolution_convert_fusion.1
  11.2 22.3 %all-gather.1 = bf16[8,1,16]{2,1,0:T(2,128)(2,1)S(1)} all-gather(bf16[1,1,16]{2,1,0:T(2,128)(2,1)S(1)} %get-tuple-element.133), channel_id=1, replica_groups=mesh['seq'=8,'head'=4] {'seq'}, dimensions={0}, use_global_device_ids=true | all-gather | bytes 288 | tf_op jit(solution)/shard_map/all_gather | solution.py:17
  33.7 1.8 convolution_bitcast_fusion.1
  35.4 52.0 %all-gather.7.cloned.1.call-done = bf16[128,128,128]{2,1,0:T(8,128)(2,1)} async-done(((bf16[16,128,128]{2,1,0:T(8,128)(2,1)}), bf16[128,128,128]{2,1,0:T(8,128)(2,1)}) %all-gather.7.cloned.1.call-update) | async-done | bytes 4194320 | tf_op jit(solution)/shard_map/all_gather | solution.py:17
  87.4 10.6 %while.14 = (s32[]{:T(128)}, f32[16,128,128]{2,1,0:T(8,128)S(1)}, s32[]{:T(128)}, bf16[8,16]{1,0:T(8,128)(2,1)S(1)}, bf16[8,16,128,128]{3,2,1,0:T(8,128)(2,1)}, /*index=5*/s32[]{:T(128)}, s32[]{:T(128)}) while((s32[]{:T(128)}, f32[16,128,128]{2,1,0:T(8,128)S(1)}, s32[]{:T(128)}, bf16[8,16]{1,0:T(8,128)(2,1)S(1)}, ...), condition=%wide.region_2.3_spmd.clone, body=%wide.region_1.2_spmd.clone.sunk | while | flops 1310740 | bytes 2621705 | solution.py:34
  98.0 2.3 multiply_reduce_fusion.1
  100.5 13.0 %convolution_convert_fusion = bf16[128,6144]{1,0:T(8,128)(2,1)} fusion(bf16[128,2048]{0,1:T(8,128)(2,1)S(1)} %bitcast.93, bf16[2048,6144]{1,0:T(8,128)(2,1)} %param.19), kind=kOutput, calls=%fused_computation.8 | convolution fusion | flops 3222011904 | bytes 27262976 | tf_op jit(solution)/shard_map/dot_general | solution.py:102
  116.1 2.4 scatter_custom_fusion
  118.5 21.5 %reduce-scatter.3.cloned.1.call-done = bf16[128,1536]{1,0:T(8,128)(2,1)} async-done(((bf16[128,6144]{1,0:T(8,128)(2,1)}), bf16[128,1536]{1,0:T(8,128)(2,1)}) %reduce-scatter.3.cloned.1.call-update) | async-done | bytes 393232 | tf_op jit(solution)/shard_map/reduce_scatter | solution.py:105
  141.3 5.8 %psum.7 = f32[128]{0:T(128)S(1)} all-reduce(f32[128]{0:T(128)S(1)} %multiply_reduce_fusion.2), channel_id=1, replica_groups=mesh['seq'=8,'head'=4] {'head'}, use_global_device_ids=true, to_apply=%region_6.7 | all-reduce | flops 128 | bytes 1024 | tf_op jit(solution)/shard_map/psum | solution.py:109
  148.3 2.2 gather_fusion
  150.7 51.2 %all_to_all.10 = bf16[8,80,1536]{2,1,0:T(8,128)(2,1)} all-to-all(bf16[8,80,1536]{2,1,0:T(8,128)(2,1)S(1)} %bitcast.91), channel_id=1, replica_groups=mesh['seq'=8,'head'=4] {'seq'}, dimensions={0} | all-to-all | bytes 3932160 | tf_op jit(solution)/shard_map/all_to_all | solution.py:122
  204.0 51.1 %all-gather.5.cloned.1.call-done = bf16[8,80,6144]{2,1,0:T(8,128)(2,1)} async-done(((bf16[8,80,1536]{2,1,0:T(8,128)(2,1)}), bf16[8,80,6144]{2,1,0:T(8,128)(2,1)}) %all-gather.5.cloned.1.call-update) | async-done | bytes 7864336 | tf_op jit(solution)/shard_map/all_gather | solution.py:126
  255.1 15.0 %convolution_multiply_fusion.1 = f32[640,1152]{1,0:T(8,128)S(1)} fusion(bf16[640,6144]{1,0:T(8,128)(2,1)} %bitcast.102, bf16[6144,1152]{1,0:T(8,128)(2,1)} %param.22, f32[]{:T(128)} %bitcast.15), kind=kOutput, calls=%fused_computation.11 | convolution fusion | flops 9060433920 | bytes 24969220 | tf_op jit(solution)/shard_map/dot_general | solution.py:128
  270.2 17.0 %fusion.2 = bf16[640,1152]{1,0:T(8,128)(2,1)S(1)} fusion(bf16[640,6144]{1,0:T(8,128)(2,1)} %bitcast.103, bf16[6144,1152]{1,0:T(8,128)(2,1)} %param.23, f32[640,1152]{1,0:T(8,128)S(1)} %convolution_multiply_fusion.1, f32[]{:T(128)} %bitcast.16), kind=kOutput, calls=%fused_computation.13 | convolution fusion | flops 9064857600 | bytes 26443780 | tf_op jit(solution)/shard_map/dot_general | solution.py:129
  287.2 12.2 %multiply_convert_fusion = bf16[640,6144]{1,0:T(8,128)(2,1)} fusion(bf16[640,1152]{1,0:T(8,128)(2,1)S(1)} %fusion.2, bf16[1152,6144]{1,0:T(8,128)(2,1)S(1)} %bitcast.101, f32[]{:T(128)} %bitcast.17), kind=kOutput, calls=%fused_computation.7 | convolution fusion | flops 9067560960 | bytes 23494660 | tf_op jit(solution)/shard_map/dot_general | solution.py:131
  299.4 69.1 %reduce-scatter.5.cloned.1.call-done = bf16[8,80,1536]{2,1,0:T(8,128)(2,1)} async-done(((bf16[8,80,6144]{2,1,0:T(8,128)(2,1)}), bf16[8,80,1536]{2,1,0:T(8,128)(2,1)}) %reduce-scatter.5.cloned.1.call-update) | async-done | bytes 1966096 | tf_op jit(solution)/shard_map/reduce_scatter | solution.py:135
  368.6 5.5 %all-to-all-start.1 = ((bf16[8,80,1536]{2,1,0:T(8,128)(2,1)}), bf16[8,80,1536]{2,1,0:T(8,128)(2,1)}, u32[]{:S(2)}, u32[]{:S(2)}) async-start(bf16[8,80,1536]{2,1,0:T(8,128)(2,1)} %reduce-scatter.5.cloned.1.call-done), calls=%async_computation.3 | async-start | bytes 3932160 | tf_op jit(solution)/shard_map/all_to_all | solution.py:141
  374.4 1.9 gather_fusion.2
  376.9 42.7 %all-to-all-done.1 = bf16[8,80,1536]{2,1,0:T(8,128)(2,1)} async-done(((bf16[8,80,1536]{2,1,0:T(8,128)(2,1)}), bf16[8,80,1536]{2,1,0:T(8,128)(2,1)}, u32[]{:S(2)}, u32[]{:S(2)}) %all-to-all-start.1) | async-done | bytes 1966112 | tf_op jit(solution)/shard_map/all_to_all | solution.py:141
  419.6 2.1 convert_reduce_fusion
  421.7 2.3 gather_fusion.1
  424.1 2.3 reshape.226
  426.4 2.2 multiply_reduce_fusion
  (88 shorter events, 19.2 us)
Async XLA Ops:
  6.5 27.1 %copy-start = (bf16[128,2048]{1,0:T(8,128)(2,1)S(1)}, bf16[128,2048]{1,0:T(8,128)(2,1)}, u32[]{:S(2)}) copy-start(bf16[128,2048]{1,0:T(8,128)(2,1)} %param.14) | copy-start | bytes 1572868
  6.5 80.9 %all-gather.7.cloned.1.call-start = ((), (), s32[]{:S(2)}) async-start(), calls=%async_computation.7 | async-start | bytes 4718592 | tf_op jit(solution)/shard_map/all_gather | solution.py:17
  11.2 128.9 %reduce-scatter.3.cloned.1.call-start = ((), (), s32[]{:S(2)}) async-start(), calls=%async_computation.4 | async-start | bytes 1966080 | tf_op jit(solution)/shard_map/reduce_scatter | solution.py:105
  100.4 13.1 %copy-start.5 = (s32[128,2]{0,1:T(2,128)S(1)}, s32[128,2]{0,1:T(2,128)}, u32[]{:S(2)}) copy-start(s32[128,2]{0,1:T(2,128)} %param.20) | copy-start | bytes 3076
  100.4 13.8 %copy-start.4 = (f32[14]{0:T(128)S(1)}, f32[14]{0:T(128)}, u32[]{:S(2)}) copy-start(f32[14]{0:T(128)} %param.25) | copy-start | bytes 172
  100.5 39.6 %copy-start.2 = (s32[128,1536]{1,0:T(8,128)S(1)}, s32[128,1536]{1,0:T(8,128)}, u32[]{:S(2)}) copy-start(s32[128,1536]{1,0:T(8,128)} %param.18) | copy-start | bytes 2359300
  113.5 141.6 %all-gather.5.cloned.1.call-start = ((), (), s32[]{:S(2)}) async-start(), calls=%async_computation.5 | async-start | bytes 9830400 | tf_op jit(solution)/shard_map/all_gather | solution.py:126
  201.9 166.7 %reduce-scatter.5.cloned.1.call-start = ((), (), s32[]{:S(2)}) async-start(), calls=%async_computation.6 | async-start | bytes 9830400 | tf_op jit(solution)/shard_map/reduce_scatter | solution.py:135
  255.1 32.1 %slice-start = ((s8[14155776]{0:T(1024)(128)(4,1)}), s8[4194304]{0:T(1024)(128)(4,1)S(1)}, s32[]{:S(2)}) async-start(s8[14155776]{0:T(1024)(128)(4,1)} %bitcast.100), calls=%async_computation.8 | async-start | bytes 8388608
  255.1 32.1 %slice-start.1 = ((s8[14155776]{0:T(1024)(128)(4,1)}), s8[4194304]{0:T(1024)(128)(4,1)S(1)}, s32[]{:S(2)}) async-start(s8[14155776]{0:T(1024)(128)(4,1)} %bitcast.100), calls=%async_computation.9 | async-start | bytes 8388608
  270.1 17.0 %slice-start.2 = ((s8[14155776]{0:T(1024)(128)(4,1)}), s8[4194304]{0:T(1024)(128)(4,1)S(1)}, s32[]{:S(2)}) async-start(s8[14155776]{0:T(1024)(128)(4,1)} %bitcast.100), calls=%async_computation.10 | async-start | bytes 8388608
  270.2 17.0 %slice-start.3 = ((s8[14155776]{0:T(1024)(128)(4,1)}), s8[1572864]{0:T(1024)(128)(4,1)S(1)}, s32[]{:S(2)}) async-start(s8[14155776]{0:T(1024)(128)(4,1)} %bitcast.100), calls=%async_computation.11 | async-start | bytes 3145728
  368.6 51.0 %all-to-all-start.1 = ((bf16[8,80,1536]{2,1,0:T(8,128)(2,1)}), bf16[8,80,1536]{2,1,0:T(8,128)(2,1)}, u32[]{:S(2)}, u32[]{:S(2)}) async-start(bf16[8,80,1536]{2,1,0:T(8,128)(2,1)} %reduce-scatter.5.cloned.1.call-done), calls=%async_computation.3 | async-start | bytes 3932160 | tf_op jit(solution)/shard_map/all_to_all | solution.py:141
  374.4 2.5 copy-start.6
  424.1 4.5 %copy-start.3 = (bf16[128,1536]{1,0:T(8,128)(2,1)S(1)}, bf16[128,1536]{1,0:T(8,128)(2,1)}, u32[]{:S(2)}) copy-start(bf16[128,1536]{1,0:T(8,128)(2,1)} %reduce-scatter.3.cloned.1.call-done) | copy-start | bytes 1179652
  424.1 5.4 %copy-start.1 = (bf16[128,2048]{1,0:T(8,128)(2,1)S(1)}, bf16[128,2048]{1,0:T(8,128)(2,1)}, u32[]{:S(2)}) copy-start(bf16[128,2048]{1,0:T(8,128)(2,1)} %param.14) | copy-start | bytes 1572868
Sparse Core Ops, SparseCore 0:
  11.3 76.0 all-gather.6
  113.6 26.4 reduce-scatter.2
  202.0 53.0 all-gather.4
  299.5 68.9 reduce-scatter.4
where the time goes:
time: 437 us; the launch traced here: 436 us
  waiting for transfers between devices  237 us (54%)
  blocking collectives  79.2 us (18%)
  matrix products  63.4 us (15%)
  other arithmetic  18.8 us (4%)
  between operations  16.6 us (4%)
  local copies, waits for them, and re-layouts  15.5 us (4%)
  starting transfers between devices  5.83 us (1%)
    reduce_scatter x1, waiting for transfers between devices, local(): lax.psum_scatter(lax.optimization_barrier(part).astype(jnp.float32).astyp...  69.1 us
    all_gather x1, waiting for transfers between devices, prefix(): lax.all_gather(part.astype(kind), axis)  52 us
    all_to_all x1, blocking collectives, local(): lax.all_to_all(pack_rows(normed, table, group), 'seq', split_axis=0, conc...  51.2 us
    all_gather x1, waiting for transfers between devices, local(): piece = lax.all_gather(received, 'head', axis=2, tiled=True)  51.1 us
    all_to_all x1, waiting for transfers between devices, local(): lax.all_to_all(summed.astype(jnp.bfloat16), 'seq', split_axis=0, concat_a...  42.7 us
    all_gather x1, blocking collectives, prefix(): lax.all_gather(part.astype(kind), axis)  22.3 us
    reduce_scatter x1, waiting for transfers between devices, local(): lax.psum_scatter(mapped_vectors.astype(jnp.bfloat16), 'head', scatter_dim...  21.5 us
    dot_general x1, matrix products, local(): up = jnp.dot(flat_rows, up_weight, preferred_element_type=jnp.float32)  17 us
  transfers between devices with their start and end apart: 5, of which 5 were waited for; matrix products, arithmetic and copies ran while one was open for 2% of the time, Pallas kernels for 0%

commit v1 on v0

--- a/solution.py
+++ b/solution.py
@@ -1,6 +1,10 @@
+import functools
+
 import jax
 import jax.numpy as jnp
 from jax import lax
+from jax.experimental import pallas as pl
+from jax.experimental.pallas import tpu as pltpu
 from jax.sharding import PartitionSpec as P
 
 D = 6144
@@ -9,6 +13,9 @@
 HEAD_DIM = 128
 EXPERTS = 4
 CAP = 80
+CORES = 2
+MESH = pl.DeviceIdType.MESH
+VMEM_LIMIT = 60 * 1024 * 1024
 
 
 def prefix(value, axis, combine, identity):
@@ -34,18 +41,419 @@
     return lax.fori_loop(0, length, hop, start)
 
 
-def pack_rows(source, table, group):
-    padded = jnp.concatenate([source, jnp.zeros((1, source.shape[1]), source.dtype)], axis=0)
-    picked = padded[table].reshape(EXPERTS, CAP, source.shape[1])
-    return jnp.repeat(picked, group, axis=0)
-
-
-def route_rows(returned, group, routes, places, route_weight):
-    width = returned.shape[2]
-    summed = jnp.sum(returned.reshape(EXPERTS, group, CAP, width), axis=1, dtype=jnp.float32)
-    chosen = jnp.take_along_axis(places, routes, axis=1)
-    picked = summed.reshape(EXPERTS * CAP, width)[routes * CAP + chosen]
-    return jnp.sum(route_weight[:, :, None] * picked, axis=1)
+def flip(value, by):
+    low, high = (lax.rem(value, 2), value // 2)
+    low = 1 - low if by % 2 else low
+    high = 1 - high if by // 2 else high
+    return low + 2 * high
+
+
+def column_tile(columns):
+    for tile in (512, 384, 256, 128):
+        if columns % tile == 0:
+            return tile
+    return columns
+
+
+class Place:
+    def __init__(self, group):
+        self.group = group
+        self.height = lax.axis_size("head") // CORES
+        seq, head = (lax.axis_index("seq"), lax.axis_index("head"))
+        self.expert, self.x = (seq // group, lax.rem(seq, group))
+        self.y, self.core = (head // CORES, lax.rem(head, CORES))
+        self.head = head
+        self.offsets = [
+            (dx, dy) for dx in range(group) for dy in range(self.height) if (dx, dy) != (0, 0)
+        ]
+        self.offsets.sort(key=lambda pair: (pair[0] != 0) + (pair[1] != 0))
+
+    def column(self, y, core):
+        return y * CORES + core
+
+    def ahead(self, dx, dy):
+        return lax.rem(self.x + dx, self.group), lax.rem(self.y + dy, self.height)
+
+    def behind(self, dx, dy):
+        return (
+            lax.rem(self.x + self.group - dx, self.group),
+            lax.rem(self.y + self.height - dy, self.height),
+        )
+
+    def partner(self):
+        return self.expert * self.group + self.x, self.column(self.y, 1 - self.core)
+
+    def plane(self, dx, dy):
+        x, y = self.ahead(dx, dy)
+        return self.expert * self.group + x, self.column(y, self.core)
+
+    def along(self, k):
+        return flip(self.expert, k) * self.group + self.x, self.head
+
+    def greet(self):
+        barrier = pltpu.get_barrier_semaphore()
+        targets = [self.partner()]
+        targets += [self.plane(dx, dy) for dx, dy in self.offsets]
+        targets += [self.along(k) for k in range(1, EXPERTS)]
+        for target in targets:
+            pl.semaphore_signal(barrier, inc=1, device_id=target, device_id_type=MESH)
+        pl.semaphore_wait(barrier, len(targets))
+
+
+def remote(source, target, send, receive, device):
+    return pltpu.make_async_remote_copy(
+        src_ref=source,
+        dst_ref=target,
+        send_sem=send,
+        recv_sem=receive,
+        device_id=device,
+        device_id_type=MESH,
+    )
+
+
+def inputs_kernel(
+    group,
+    scale_ref,
+    packed_ref,
+    gate_ref,
+    up_ref,
+    act_ref,
+    rows,
+    gate_held,
+    up_held,
+    gate_sum,
+    up_sum,
+    arrived,
+    sent_along,
+    sent_plane,
+    sent_core,
+    loaded,
+    local_sem,
+):
+    at = Place(group)
+    width = packed_ref.shape[2]
+    columns = gate_ref.shape[1]
+    tile = column_tile(columns)
+    partner = at.partner()
+    count = len(at.offsets)
+    order = []
+    for dy in range(at.height):
+        y = lax.rem(at.y + dy, at.height)
+        order += [at.column(y, at.core), at.column(y, 1 - at.core)]
+
+    loads = []
+    for step, head in enumerate(order):
+        part = pl.ds(pl.multiple_of(head * width, width), width)
+        loads.append(
+            (
+                pltpu.make_async_copy(gate_ref.at[part], gate_held.at[part], loaded.at[0, step]),
+                pltpu.make_async_copy(up_ref.at[part], up_held.at[part], loaded.at[1, step]),
+            )
+        )
+        loads[-1][0].start()
+        loads[-1][1].start()
+    own = pltpu.make_async_copy(packed_ref.at[at.expert], rows.at[at.head, 0, at.x], local_sem)
+    own.start()
+    at.greet()
+
+    started = []
+
+    def push(source, head, k, x, send, device):
+        copy = remote(source, rows.at[head, k, x], send, arrived.at[head, k, x], device)
+        copy.start()
+        started.append(copy)
+
+    def landed(head, k, x):
+        block = rows.at[head, k, x]
+        remote(block, block, sent_along.at[0], arrived.at[head, k, x], partner).wait_recv()
+
+    for k in (1, 2, 3):
+        push(packed_ref.at[flip(at.expert, k)], at.head, k, at.x, sent_along.at[k - 1], at.along(k))
+    own.wait()
+
+    def launch(k):
+        if k:
+            landed(at.head, k, at.x)
+        block = rows.at[at.head, k, at.x]
+        for number, (dx, dy) in enumerate(at.offsets):
+            push(block, at.head, k, at.x, sent_plane.at[k, number], at.plane(dx, dy))
+        push(block, at.head, k, at.x, sent_core.at[k, count], partner)
+
+    def relay(k):
+        for number, (dx, dy) in enumerate(at.offsets):
+            x, y = at.behind(dx, dy)
+            head = at.column(y, at.core)
+            landed(head, k, x)
+            push(rows.at[head, k, x], head, k, x, sent_core.at[k, number], partner)
+
+    def multiply(phase, step):
+        head = order[step]
+        for k in (2 * phase, 2 * phase + 1):
+            if step % 2:
+                for x in range(group):
+                    landed(head, k, x)
+        if phase == 0:
+            loads[step][0].wait()
+            loads[step][1].wait()
+        depth = pl.ds(pl.multiple_of(head * width, width), width)
+
+        def body(index, carry):
+            if tile == columns:
+                part = slice(None)
+            else:
+                part = pl.ds(pl.multiple_of(index * tile, tile), tile)
+            block = rows[head, 2 * phase : 2 * phase + 2].reshape(gate_sum.shape[0], width)
+            for held, total in ((gate_held, gate_sum), (up_held, up_sum)):
+                product = jnp.dot(block, held[depth, part], preferred_element_type=jnp.float32)
+                if step == 0:
+                    total[:, part] = product
+                else:
+                    total[:, part] += product
+            return carry
+
+        lax.fori_loop(0, columns // tile, body, 0)
+
+    def activate(phase):
+        block_rows = gate_sum.shape[0] // 2
+        for half in range(2):
+            inner = slice(half * block_rows, (half + 1) * block_rows)
+            gate = gate_sum[inner, :] * scale_ref[0]
+            up = up_sum[inner, :] * scale_ref[1]
+            value = gate / (1.0 + jnp.exp(-gate)) * up
+            act_ref[2 * phase + half] = value.astype(jnp.bfloat16)
+
+    launch(0)
+    launch(1)
+    relay(0)
+    launch(2)
+    relay(1)
+    launch(3)
+    half = len(order) // 2
+    for step in range(len(order)):
+        if step == half:
+            relay(2)
+        multiply(0, step)
+    activate(0)
+    relay(3)
+    for step in range(len(order)):
+        multiply(1, step)
+    activate(1)
+    for copy in started:
+        copy.wait_send()
+
+
+def expert_inputs(factors, packed, gate_weight, up_weight, group):
+    experts, cap, width = packed.shape
+    heads = lax.axis_size("head")
+    depth, columns = gate_weight.shape
+    others = group * heads // CORES - 1
+    half = experts * group * cap // 2
+    vmem = pl.BlockSpec(memory_space=pltpu.VMEM)
+    return pl.pallas_call(
+        functools.partial(inputs_kernel, group),
+        out_shape=jax.ShapeDtypeStruct((experts, group * cap, columns), jnp.bfloat16),
+        in_specs=[
+            pl.BlockSpec(memory_space=pltpu.SMEM),
+            vmem,
+            pl.BlockSpec(memory_space=pl.ANY),
+            pl.BlockSpec(memory_space=pl.ANY),
+        ],
+        out_specs=vmem,
+        scratch_shapes=[
+            pltpu.VMEM((heads, experts, group, cap, width), jnp.bfloat16),
+            pltpu.VMEM((depth, columns), jnp.bfloat16),
+            pltpu.VMEM((depth, columns), jnp.bfloat16),
+            pltpu.VMEM((half, columns), jnp.float32),
+            pltpu.VMEM((half, columns), jnp.float32),
+            pltpu.SemaphoreType.DMA((heads, experts, group)),
+            pltpu.SemaphoreType.DMA((experts - 1,)),
+            pltpu.SemaphoreType.DMA((experts, others)),
+            pltpu.SemaphoreType.DMA((experts, others + 1)),
+            pltpu.SemaphoreType.DMA((2, heads)),
+            pltpu.SemaphoreType.DMA,
+        ],
+        compiler_params=pltpu.CompilerParams(
+            collective_id=1, has_side_effects=True, vmem_limit_bytes=VMEM_LIMIT
+        ),
+    )(factors, packed, gate_weight, up_weight)
+
+
+SEND_ORDER = (2, 3, 1, 0)
+
+
+def outputs_kernel(
+    group,
+    scale_ref,
+    act_ref,
+    down_ref,
+    returned_ref,
+    held,
+    outgoing,
+    incoming,
+    sums,
+    landing,
+    finished,
+    core_sent,
+    core_arrived,
+    plane_sent,
+    plane_arrived,
+    along_sent,
+    along_arrived,
+    loaded,
+):
+    at = Place(group)
+    width = returned_ref.shape[2]
+    cap = returned_ref.shape[1]
+    tile = column_tile(width)
+    partner = at.partner()
+    height = at.height
+    turns = list(range(height - 1, -1, -1))
+
+    def columns_of(turn, mine):
+        y = lax.rem(at.y + turn, height)
+        return at.column(y, at.core if mine else 1 - at.core)
+
+    loads = {}
+    for place, turn in enumerate(turns):
+        for mine in (0, 1):
+            part = pl.ds(pl.multiple_of(columns_of(turn, mine) * width, width), width)
+            copy = pltpu.make_async_copy(
+                down_ref.at[:, part], held.at[:, part], loaded.at[place, mine]
+            )
+            copy.start()
+            loads[turn, mine] = copy
+    at.greet()
+    started = []
+
+    def product(turn, mine, target):
+        loads[turn, mine].wait()
+        first = columns_of(turn, mine) * width
+
+        def body(index, carry):
+            part = pl.ds(pl.multiple_of(first + index * tile, tile), tile)
+            inner = pl.ds(pl.multiple_of(index * tile, tile), tile)
+            for pair in range(2):
+                rows = act_ref[2 * pair : 2 * pair + 2].reshape(2 * group * cap, act_ref.shape[2])
+                value = jnp.dot(rows, held[:, part], preferred_element_type=jnp.float32)
+                value = (value * scale_ref[0]).astype(jnp.bfloat16)
+                target[turn, 2 * pair : 2 * pair + 2, :, :, inner] = value.reshape(
+                    2, group, cap, tile
+                )
+            return carry
+
+        lax.fori_loop(0, width // tile, body, 0)
+
+    def core_copy(turn):
+        return remote(
+            outgoing.at[turn],
+            incoming.at[turn],
+            core_sent.at[turn],
+            core_arrived.at[turn],
+            partner,
+        )
+
+    def plane_copy(number, k, source, device):
+        return remote(
+            source,
+            landing.at[number, k],
+            plane_sent.at[number, k],
+            plane_arrived.at[number, k],
+            device,
+        )
+
+    def join(turn):
+        core_copy(turn).wait_recv()
+        offsets = [pair for pair in at.offsets if pair[1] == turn]
+        offsets.sort(key=lambda pair: -pair[0])
+        for k in SEND_ORDER:
+            for x in range(group):
+                sums[turn, k, x] = (
+                    sums[turn, k, x].astype(jnp.float32) + incoming[turn, k, x].astype(jnp.float32)
+                ).astype(jnp.bfloat16)
+            for dx, dy in offsets:
+                x, _ = at.ahead(dx, dy)
+                copy = plane_copy(
+                    at.offsets.index((dx, dy)), k, sums.at[turn, k, x], at.plane(dx, dy)
+                )
+                copy.start()
+                started.append(copy)
+
+    previous = None
+    for turn in turns:
+        product(turn, 0, outgoing)
+        copy = core_copy(turn)
+        copy.start()
+        started.append(copy)
+        if previous is not None:
+            join(previous)
+        product(turn, 1, sums)
+        previous = turn
+    join(previous)
+    for k in SEND_ORDER:
+        total = sums[0, k, at.x].astype(jnp.float32)
+        for number, (dx, dy) in enumerate(at.offsets):
+            plane_copy(number, k, landing.at[number, k], partner).wait_recv()
+            total = total + landing[number, k].astype(jnp.float32)
+        if k == 0:
+            returned_ref[at.expert] = total.astype(jnp.bfloat16)
+        else:
+            finished[k - 1] = total.astype(jnp.bfloat16)
+            copy = remote(
+                finished.at[k - 1],
+                returned_ref.at[at.expert],
+                along_sent.at[k - 1],
+                along_arrived.at[k - 1],
+                at.along(k),
+            )
+            copy.start()
+            started.append(copy)
+    for k in (1, 2, 3):
+        block = returned_ref.at[flip(at.expert, k)]
+        remote(
+            finished.at[k - 1], block, along_sent.at[k - 1], along_arrived.at[k - 1], at.along(k)
+        ).wait_recv()
+    for copy in started:
+        copy.wait_send()
+
+
+def expert_outputs(factor, act, down_weight, group):
+    experts, cap, columns = act.shape
+    cap = cap // group
+    heads = lax.axis_size("head")
+    depth, features = down_weight.shape
+    width = features // heads
+    height = heads // CORES
+    others = group * height - 1
+    vmem = pl.BlockSpec(memory_space=pltpu.VMEM)
+    block = (height, experts, group, cap, width)
+    return pl.pallas_call(
+        functools.partial(outputs_kernel, group),
+        out_shape=jax.ShapeDtypeStruct((experts, cap, width), jnp.bfloat16),
+        in_specs=[
+            pl.BlockSpec(memory_space=pltpu.SMEM),
+            vmem,
+            pl.BlockSpec(memory_space=pl.ANY),
+        ],
+        out_specs=vmem,
+        scratch_shapes=[
+            pltpu.VMEM((depth, features), jnp.bfloat16),
+            pltpu.VMEM(block, jnp.bfloat16),
+            pltpu.VMEM(block, jnp.bfloat16),
+            pltpu.VMEM(block, jnp.bfloat16),
+            pltpu.VMEM((others, experts, cap, width), jnp.bfloat16),
+            pltpu.VMEM((experts - 1, cap, width), jnp.bfloat16),
+            pltpu.SemaphoreType.DMA((height,)),
+            pltpu.SemaphoreType.DMA((height,)),
+            pltpu.SemaphoreType.DMA((others, experts)),
+            pltpu.SemaphoreType.DMA((others, experts)),
+            pltpu.SemaphoreType.DMA((experts - 1,)),
+            pltpu.SemaphoreType.DMA((experts - 1,)),
+            pltpu.SemaphoreType.DMA((height, 2)),
+        ],
+        compiler_params=pltpu.CompilerParams(
+            collective_id=2, has_side_effects=True, vmem_limit_bytes=VMEM_LIMIT
+        ),
+    )(factor, act, down_weight)
 
 
 def combine_states(earlier, later):
@@ -113,35 +521,32 @@
         jnp.int32
     )
     places = jnp.cumsum(hits, axis=0, dtype=jnp.int32) - hits
-    target = jnp.where(hits > 0, expert_ids * CAP + places, EXPERTS * CAP).reshape(-1)
-    sources = lax.broadcasted_iota(jnp.int32, (tokens, EXPERTS), 0).reshape(-1)
-    table = jnp.full((EXPERTS * CAP,), tokens, jnp.int32).at[target].set(sources, mode="drop")
+    slots = lax.broadcasted_iota(jnp.int32, (EXPERTS, CAP, tokens), 1)
+    picks = jnp.logical_and(places.T[:, None, :] == slots, hits.T[:, None, :] > 0)
+    packed = jnp.dot(
+        picks.reshape(EXPERTS * CAP, tokens).astype(jnp.bfloat16),
+        normed,
+        preferred_element_type=jnp.float32,
+    ).astype(jnp.bfloat16)
     gate_scale = scales[2 + owner] * D ** (-0.5)
     up_scale = scales[2 + EXPERTS + owner] * D ** (-0.5)
     down_scale = scales[2 + 2 * EXPERTS + owner] * FF ** (-0.5)
-    received = lax.all_to_all(
-        pack_rows(normed, table, group), "seq", split_axis=0, concat_axis=0, tiled=True
-    )
-    count = received.shape[1]
-    piece = lax.all_gather(received, "head", axis=2, tiled=True)
-    flat_rows = piece.reshape(sequence_count * count, piece.shape[2])
-    gate = jnp.dot(flat_rows, gate_weight, preferred_element_type=jnp.float32)
-    up = jnp.dot(flat_rows, up_weight, preferred_element_type=jnp.float32)
-    act = (jax.nn.silu(gate * gate_scale) * (up * up_scale)).astype(jnp.bfloat16)
-    part = (jnp.dot(act, down_weight, preferred_element_type=jnp.float32) * down_scale).astype(
-        jnp.bfloat16
-    )
-    part = part.reshape(sequence_count, count, down_weight.shape[1])
-    summed = lax.psum_scatter(
-        lax.optimization_barrier(part).astype(jnp.float32).astype(jnp.bfloat16),
-        "head",
-        scatter_dimension=2,
-        tiled=True,
-    ).astype(jnp.float32)
-    returned = lax.all_to_all(
-        summed.astype(jnp.bfloat16), "seq", split_axis=0, concat_axis=0, tiled=True
-    ).astype(summed.dtype)
-    moe = route_rows(returned, group, routes, places, route_weight)
+    act = expert_inputs(
+        jnp.stack([gate_scale, up_scale]),
+        packed.reshape(EXPERTS, CAP, packed.shape[1]),
+        gate_weight,
+        up_weight,
+        group,
+    )
+    returned = expert_outputs(down_scale.reshape(1), act, down_weight, group)
+    flat = returned.reshape(EXPERTS * CAP, returned.shape[2])
+    chosen = routes * CAP + jnp.take_along_axis(places, routes, axis=1)
+    lanes = lax.broadcasted_iota(jnp.int32, (tokens, EXPERTS * CAP), 1)
+    moe = 0.0
+    for route in range(routes.shape[1]):
+        one_hot = (chosen[:, route : route + 1] == lanes).astype(jnp.bfloat16)
+        picked = jnp.dot(one_hot, flat, preferred_element_type=jnp.float32)
+        moe = moe + route_weight[:, route : route + 1] * picked
     return (resid + moe).astype(jnp.bfloat16)
 
 

time: 437 us -> 294 us (0.67)
  waiting for transfers between devices: 237 us -> 71 us
  Pallas kernels: 0 us -> 132 us
  blocking collectives: 79.2 us -> 28.2 us
  matrix products: 63.4 us -> 25.5 us
  local copies, waits for them, and re-layouts: 15.5 us -> 5.64 us
  starting transfers between devices: 5.83 us -> 0.04 us
  other arithmetic: 18.8 us -> 13.1 us
    pallas_call x0 -> x2, Pallas kernels: none -> 132 us  [the longest x1 66.1 us: expert_inputs(): pl.pallas_call(functools.partial(inputs_kernel, group), out_shape=jax.Sha...]
    reduce_scatter x1 -> x0, waiting for transfers between devices: 69.1 us -> none  [local(): lax.psum_scatter(lax.optimization_barrier(part).astype(jnp.float32).astyp...]
    all_to_all x1 -> x0, blocking collectives: 51.2 us -> none  [local(): lax.all_to_all(pack_rows(normed, table, group), 'seq', split_axis=0, conc...]
    all_gather x1 -> x0, waiting for transfers between devices: 51.1 us -> none  [local(): piece = lax.all_gather(received, 'head', axis=2, tiled=True)]
    all_to_all x1 -> x0, waiting for transfers between devices: 42.7 us -> none  [local(): lax.all_to_all(summed.astype(jnp.bfloat16), 'seq', split_axis=0, concat_a...]
    dot_general x3, matrix products: 44.2 us -> 6.44 us  [the longest x2 4 us: local(): picked = jnp.dot(one_hot, flat, preferred_element_type=jnp.float32)]
    gather x8 -> x5, local copies, waits for them, and re-layouts: 9.26 us -> 2.39 us  [local(): chosen = routes * CAP + jnp.take_along_axis(places, routes, axis=1)]
    all_to_all x1 -> x0, starting transfers between devices: 5.52 us -> none  [local(): lax.all_to_all(summed.astype(jnp.bfloat16), 'seq', split_axis=0, concat_a...]
  transfers between devices with their start and end apart: 5 -> 2, of which waited for: 5 -> 2; matrix products, arithmetic and copies ran while one was open for 2% -> 2% of each run, Pallas kernels for 0% -> 0%
where the time goes in v1:
time: 294 us; the launch traced here: 293 us
  Pallas kernels  132 us (45%)
  waiting for transfers between devices  71 us (24%)
  blocking collectives  28.2 us (10%)
  matrix products  25.5 us (9%)
  between operations  16.8 us (6%)
  other arithmetic  13.1 us (4%)
  local copies, waits for them, and re-layouts  5.64 us (2%)
    pallas_call x1, Pallas kernels, expert_inputs(): pl.pallas_call(functools.partial(inputs_kernel, group), out_shape=jax.Sha...  66.1 us
    pallas_call x1, Pallas kernels, expert_outputs(): pl.pallas_call(functools.partial(outputs_kernel, group), out_shape=jax.Sh...  66.1 us
    all_gather x1, waiting for transfers between devices, prefix(): lax.all_gather(part.astype(kind), axis)  52 us
    all_gather x1, blocking collectives, prefix(): lax.all_gather(part.astype(kind), axis)  22.3 us
    reduce_scatter x1, waiting for transfers between devices, local(): lax.psum_scatter(mapped_vectors.astype(jnp.bfloat16), 'head', scatter_dim...  19 us
    dot_general x1, matrix products, local(): jnp.dot(heads_out.reshape(tokens, heads * HEAD_DIM), out_weight, preferre...  12.9 us
    select_n x8, other arithmetic, hop(): return jax.tree.map(lambda a, b: jnp.where(reached, a, b), new, before)  10.3 us
    psum x1, blocking collectives, local(): squares = lax.psum(jnp.sum(resid * resid, axis=1), 'head')  5.94 us
  transfers between devices with their start and end apart: 2, of which 2 were waited for; matrix products, arithmetic and copies ran while one was open for 2% of the time, Pallas kernels for 0%

profile of v1, /device:TPU:0, one launch (start us, length us, event | category | flops | bytes accessed | tf_op | source)
XLA Modules:
  0.0 292.7 jit_solution(2691941091690478893)
XLA Ops:
  7.7 1.3 copy.103
  9.0 2.2 convolution_convert_fusion.2
  11.2 22.3 %all-gather.1 = bf16[8,1,16]{2,1,0:T(2,128)(2,1)S(1)} all-gather(bf16[1,1,16]{2,1,0:T(2,128)(2,1)S(1)} %get-tuple-element.131), channel_id=1, replica_groups=mesh['seq'=8,'head'=4] {'seq'}, dimensions={0}, use_global_device_ids=true | all-gather | bytes 288 | tf_op jit(solution)/shard_map/all_gather | solution.py:24
  33.7 1.8 convolution_bitcast_fusion.1
  35.4 52.0 %all-gather.4.cloned.1.call-done = bf16[128,128,128]{2,1,0:T(8,128)(2,1)} async-done(((bf16[16,128,128]{2,1,0:T(8,128)(2,1)}), bf16[128,128,128]{2,1,0:T(8,128)(2,1)}) %all-gather.4.cloned.1.call-update) | async-done | bytes 4194320 | tf_op jit(solution)/shard_map/all_gather | solution.py:24
  87.4 10.6 %while.14 = (s32[]{:T(128)}, f32[16,128,128]{2,1,0:T(8,128)S(1)}, s32[]{:T(128)}, bf16[8,16]{1,0:T(8,128)(2,1)S(1)}, bf16[8,16,128,128]{3,2,1,0:T(8,128)(2,1)}, /*index=5*/s32[]{:T(128)}, s32[]{:T(128)}) while((s32[]{:T(128)}, f32[16,128,128]{2,1,0:T(8,128)S(1)}, s32[]{:T(128)}, bf16[8,16]{1,0:T(8,128)(2,1)S(1)}, ...), condition=%wide.region_2.3_spmd.clone, body=%wide.region_1.2_spmd.clone.sunk | while | flops 1310740 | bytes 2621705 | solution.py:41
  87.4 1.3 fusion.52
  88.8 1.3 fusion.52
  90.1 1.3 fusion.52
  91.4 1.3 fusion.52
  92.7 1.3 fusion.52
  94.1 1.3 fusion.52
  95.4 1.3 fusion.52
  96.7 1.3 fusion.52
  98.0 2.3 multiply_reduce_fusion
  100.5 12.9 %convolution_convert_fusion = bf16[128,6144]{1,0:T(8,128)(2,1)} fusion(bf16[128,2048]{0,1:T(8,128)(2,1)S(1)} %bitcast.95, bf16[2048,6144]{1,0:T(8,128)(2,1)} %param.19), kind=kOutput, calls=%fused_computation.4 | convolution fusion | flops 3222011904 | bytes 27262976 | tf_op jit(solution)/shard_map/dot_general | solution.py:510
  116.2 1.9 gather_fusion
  121.1 19.0 %reduce-scatter.2.cloned.1.call-done = bf16[128,1536]{1,0:T(8,128)(2,1)} async-done(((bf16[128,6144]{1,0:T(8,128)(2,1)}), bf16[128,1536]{1,0:T(8,128)(2,1)}) %reduce-scatter.2.cloned.1.call-update) | async-done | bytes 393232 | tf_op jit(solution)/shard_map/reduce_scatter | solution.py:513
  141.3 5.9 %psum.7 = f32[128]{0:T(128)S(1)} all-reduce(f32[128]{0:T(128)S(1)} %multiply_reduce_fusion.1), channel_id=1, replica_groups=mesh['seq'=8,'head'=4] {'head'}, use_global_device_ids=true, to_apply=%region_7.8 | all-reduce | flops 128 | bytes 1024 | tf_op jit(solution)/shard_map/psum | solution.py:517
  147.2 2.4 convolution_convert_fusion.1
  149.7 66.1 %shard_map.118.act_ref = bf16[4,160,1152]{2,1,0:T(8,128)(2,1)} custom-call(f32[2]{0:T(128)} %pad_maximum_fusion.scale_ref, bf16[4,80,1536]{2,1,0:T(8,128)(2,1)} %bitcast.94, bf16[6144,1152]{1,0:T(8,128)(2,1)} %gate_ref.1, bf16[6144,1152]{1,0:T(8,128)(2,1)} %up_ref.1), custom_call_target="tpu_custom_call" | custom-call | tf_op jit(solution)/shard_map/pallas_call | solution.py:252
  215.8 66.1 %shard_map.119 = bf16[4,80,1536]{2,1,0:T(8,128)(2,1)} custom-call(f32[1]{0:T(128)S(6)} %mul.138.scale_ref, bf16[4,160,1152]{2,1,0:T(8,128)(2,1)} %shard_map.118.act_ref, bf16[1152,6144]{1,0:T(8,128)(2,1)} %down_ref.1), custom_call_target="tpu_custom_call" | custom-call | tf_op jit(solution)/shard_map/pallas_call | solution.py:429
  281.9 1.6 convolution_multiply_fusion.1
  283.5 2.4 fusion.3
  (60 shorter events, 5.2 us)
Async XLA Ops:
  6.5 27.1 %copy-start = (bf16[128,2048]{1,0:T(8,128)(2,1)S(1)}, bf16[128,2048]{1,0:T(8,128)(2,1)}, u32[]{:S(2)}) copy-start(bf16[128,2048]{1,0:T(8,128)(2,1)} %param.14) | copy-start | bytes 1572868
  6.5 80.9 %all-gather.4.cloned.1.call-start = ((), (), s32[]{:S(2)}) async-start(), calls=%async_computation.2 | async-start | bytes 4718592 | tf_op jit(solution)/shard_map/all_gather | solution.py:24
  11.2 128.9 %reduce-scatter.2.cloned.1.call-start = ((), (), s32[]{:S(2)}) async-start(), calls=%async_computation.1 | async-start | bytes 1966080 | tf_op jit(solution)/shard_map/reduce_scatter | solution.py:513
  100.4 13.0 %copy-start.5 = (s32[128,2]{0,1:T(2,128)S(1)}, s32[128,2]{0,1:T(2,128)}, u32[]{:S(2)}) copy-start(s32[128,2]{0,1:T(2,128)} %param.20) | copy-start | bytes 3076
  100.4 13.4 %copy-start.4 = (f32[14]{0:T(128)S(1)}, f32[14]{0:T(128)}, u32[]{:S(2)}) copy-start(f32[14]{0:T(128)} %param.25) | copy-start | bytes 172
  116.2 4.8 %copy-start.6 = (f32[128,2]{0,1:T(2,128)S(1)}, f32[128,2]{0,1:T(2,128)}, u32[]{:S(2)}) copy-start(f32[128,2]{0,1:T(2,128)} %param.21) | copy-start | bytes 3076
  116.2 23.8 %copy-start.2 = (s32[128,1536]{1,0:T(8,128)S(1)}, s32[128,1536]{1,0:T(8,128)}, u32[]{:S(2)}) copy-start(s32[128,1536]{1,0:T(8,128)} %param.18) | copy-start | bytes 2359300
  149.7 136.2 %copy-start.1 = (bf16[128,2048]{1,0:T(8,128)(2,1)S(1)}, bf16[128,2048]{1,0:T(8,128)(2,1)}, u32[]{:S(2)}) copy-start(bf16[128,2048]{1,0:T(8,128)(2,1)} %param.14) | copy-start | bytes 1572868
  215.8 67.7 %copy-start.3 = (bf16[128,1536]{1,0:T(8,128)(2,1)S(1)}, bf16[128,1536]{1,0:T(8,128)(2,1)}, u32[]{:S(2)}) copy-start(bf16[128,1536]{1,0:T(8,128)(2,1)} %reduce-scatter.2.cloned.1.call-done) | copy-start | bytes 1179652
Sparse Core Ops, SparseCore 0:
  11.3 76.0 all-gather.3
  113.5 26.4 reduce-scatter.1

commit v2 on v1

--- a/solution.py
+++ b/solution.py
@@ -18,27 +18,23 @@
 VMEM_LIMIT = 60 * 1024 * 1024
 
 
-def prefix(value, axis, combine, identity):
-    length, mine = (lax.axis_size(axis), lax.axis_index(axis))
-    everything = jax.tree.map(
-        lambda part, kind: lax.all_gather(part.astype(kind), axis),
-        value,
-        (jnp.bfloat16, jnp.bfloat16),
-    )
-    start = jax.tree.map(
-        lambda part, zero: jnp.broadcast_to(jnp.asarray(zero, part.dtype), part.shape),
-        value,
-        identity,
-    )
-
-    def hop(k, before):
-        reached = k < mine
-        new = combine(
-            before, jax.tree.map(lambda part, own: part[k].astype(own.dtype), everything, value)
-        )
-        return jax.tree.map(lambda a, b: jnp.where(reached, a, b), new, before)
-
-    return lax.fori_loop(0, length, hop, start)
+def carried_states(decay, state, axis):
+    parts = lax.axis_size(axis)
+    flat = state.astype(jnp.bfloat16).reshape(parts, -1, HEAD_DIM)
+    rows = flat.shape[1]
+    factors = jnp.repeat(decay, state.shape[1]).reshape(parts, rows)
+    unit = 16 * HEAD_DIM
+    factors = jnp.pad(factors, ((0, 0), (0, -rows % unit))).reshape(parts, -1, HEAD_DIM)
+    sent = jnp.concatenate([flat, factors.astype(jnp.bfloat16)], axis=1)
+    blocks = lax.all_to_all(sent, axis, split_axis=0, concat_axis=0, tiled=True)
+    steps = blocks[:, :rows].astype(jnp.float32)
+    fades = blocks[:, rows:].reshape(parts, -1)[:, :rows].astype(jnp.float32)
+    carried, before = jnp.zeros_like(steps[0]), []
+    for k in range(parts):
+        before.append(carried.astype(jnp.bfloat16))
+        carried = fades[k][:, None] * carried + steps[k]
+    back = lax.all_to_all(jnp.stack(before), axis, split_axis=0, concat_axis=0, tiled=True)
+    return back.reshape(state.shape).astype(jnp.float32)
 
 
 def flip(value, by):
@@ -456,10 +452,6 @@
     )(factor, act, down_weight)
 
 
-def combine_states(earlier, later):
-    return (earlier[0] * later[0], later[0][:, None, None] * earlier[1] + later[1])
-
-
 def local(
     queries,
     memory_keys,
@@ -498,8 +490,7 @@
         key_rows.astype(jnp.float32) * jnp.exp(total[None, :] - cumulative)[:, :, None]
     ).astype(jnp.bfloat16)
     state = jnp.einsum("shd,she->hde", decayed, value_rows, preferred_element_type=jnp.float32)
-    identity = (jnp.ones_like(total), jnp.zeros_like(state))
-    carried = prefix((jnp.exp(total), state), "seq", combine_states, identity)[1]
+    carried = carried_states(jnp.exp(total), state, "seq")
     lifted = query_rows.astype(jnp.float32) * jnp.exp(cumulative)[:, :, None]
     across = jnp.einsum("thd,hde->the", lifted, carried, precision=lax.Precision.HIGHEST)
     mixer_output = inside + across

time: 294 us -> 255 us (0.87)
  blocking collectives: 28.2 us -> 5.94 us
  waiting for transfers between devices: 71 us -> 48.8 us
  starting transfers between devices: 0.04 us -> 10.9 us
  other arithmetic: 13.1 us -> 8.87 us
    all_gather x1 -> x0, waiting for transfers between devices: 52 us -> none  [prefix(): lax.all_gather(part.astype(kind), axis)]
    all_to_all x0 -> x2, waiting for transfers between devices: none -> 29 us  [the longest x1 14.6 us: carried_states(): blocks = lax.all_to_all(sent, axis, split_axis=0, concat_axis=0, tiled=True)]
    all_gather x1 -> x0, blocking collectives: 22.3 us -> none  [prefix(): lax.all_gather(part.astype(kind), axis)]
    all_to_all x0 -> x2, starting transfers between devices: none -> 10.9 us  [the longest x1 7.25 us: carried_states(): blocks = lax.all_to_all(sent, axis, split_axis=0, concat_axis=0, tiled=True)]
    select_n x8 -> x0, other arithmetic: 10.3 us -> none  [hop(): return jax.tree.map(lambda a, b: jnp.where(reached, a, b), new, before)]
    unnamed x1 -> x6, other arithmetic: 0.01 us -> 4.44 us
  transfers between devices with their start and end apart: 2 -> 3, of which waited for: 2 -> 3; matrix products, arithmetic and copies ran while one was open for 2% -> 2% of each run, Pallas kernels for 0% -> 0%
where the time goes in v2:
time: 255 us; the launch traced here: 254 us
  Pallas kernels  132 us (52%)
  waiting for transfers between devices  48.8 us (19%)
  matrix products  23.9 us (9%)
  between operations  16.9 us (7%)
  starting transfers between devices  10.9 us (4%)
  other arithmetic  8.87 us (3%)
  local copies, waits for them, and re-layouts  6.54 us (3%)
  blocking collectives  5.94 us (2%)
    pallas_call x1, Pallas kernels, expert_outputs(): pl.pallas_call(functools.partial(outputs_kernel, group), out_shape=jax.Sh...  66.1 us
    pallas_call x1, Pallas kernels, expert_inputs(): pl.pallas_call(functools.partial(inputs_kernel, group), out_shape=jax.Sha...  66.1 us
    reduce_scatter x1, waiting for transfers between devices, local(): lax.psum_scatter(mapped_vectors.astype(jnp.bfloat16), 'head', scatter_dim...  19.7 us
    all_to_all x1, waiting for transfers between devices, carried_states(): blocks = lax.all_to_all(sent, axis, split_axis=0, concat_axis=0, tiled=True)  14.6 us
    all_to_all x1, waiting for transfers between devices, carried_states(): lax.all_to_all(jnp.stack(before), axis, split_axis=0, concat_axis=0, tile...  14.5 us
    dot_general x1, matrix products, local(): jnp.dot(heads_out.reshape(tokens, heads * HEAD_DIM), out_weight, preferre...  12.9 us
    all_to_all x1, starting transfers between devices, carried_states(): blocks = lax.all_to_all(sent, axis, split_axis=0, concat_axis=0, tiled=True)  7.25 us
    psum x1, blocking collectives, local(): squares = lax.psum(jnp.sum(resid * resid, axis=1), 'head')  5.94 us
  transfers between devices with their start and end apart: 3, of which 3 were waited for; matrix products, arithmetic and copies ran while one was open for 2% of the time, Pallas kernels for 0%

profile of v2, /device:TPU:0, one launch (start us, length us, event | category | flops | bytes accessed | tf_op | source)
XLA Modules:
  0.0 254.0 jit_solution(8119197320718352375)
XLA Ops:
  6.5 0.9 copy.69
  8.0 1.3 copy.84
  9.6 0.8 pad_maximum_fusion
  10.5 7.3 %all-to-all-start = ((bf16[8,272,128]{2,1,0:T(8,128)(2,1)}), bf16[8,272,128]{2,1,0:T(8,128)(2,1)S(1)}, u32[]{:S(2)}, u32[]{:S(2)}) async-start(bf16[8,272,128]{2,1,0:T(8,128)(2,1)} %pad_maximum_fusion), calls=%async_computation | async-start | bytes 1114112 | tf_op jit(solution)/shard_map/all_to_all | solution.py:29
  18.3 14.6 %all-to-all-done = bf16[8,272,128]{2,1,0:T(8,128)(2,1)S(1)} async-done(((bf16[8,272,128]{2,1,0:T(8,128)(2,1)}), bf16[8,272,128]{2,1,0:T(8,128)(2,1)S(1)}, u32[]{:S(2)}, u32[]{:S(2)}) %all-to-all-start) | async-done | bytes 557088 | tf_op jit(solution)/shard_map/all_to_all | solution.py:29
  33.8 0.7 convert_dynamic-update-slice_fusion.4
  35.2 0.8 convert_dynamic-update-slice_fusion.2
  36.0 0.7 convert_dynamic-update-slice_fusion.1
  36.7 0.7 convert_dynamic-update-slice_fusion
  37.5 0.7 fusion.34
  38.2 3.6 %all-to-all-start.1 = ((bf16[8,256,128]{2,1,0:T(8,128)(2,1)}), bf16[8,256,128]{2,1,0:T(8,128)(2,1)S(1)}, u32[]{:S(2)}, u32[]{:S(2)}) async-start(bf16[8,256,128]{2,1,0:T(8,128)(2,1)} %fusion.34), calls=%async_computation.1 | async-start | bytes 1048576 | tf_op jit(solution)/shard_map/all_to_all | solution.py:36
  42.0 14.5 %all-to-all-done.1 = bf16[8,256,128]{2,1,0:T(8,128)(2,1)S(1)} async-done(((bf16[8,256,128]{2,1,0:T(8,128)(2,1)}), bf16[8,256,128]{2,1,0:T(8,128)(2,1)S(1)}, u32[]{:S(2)}, u32[]{:S(2)}) %all-to-all-start.1) | async-done | bytes 524320 | tf_op jit(solution)/shard_map/all_to_all | solution.py:36
  56.5 2.5 convolution_bitcast_fusion.1
  59.0 1.8 multiply_reduce_fusion
  60.9 12.9 %convolution_convert_fusion = bf16[128,6144]{1,0:T(8,128)(2,1)} fusion(bf16[128,2048]{0,1:T(8,128)(2,1)S(1)} %bitcast.102, bf16[2048,6144]{1,0:T(8,128)(2,1)} %param.17), kind=kOutput, calls=%fused_computation.1 | convolution fusion | flops 3222011904 | bytes 27262976 | tf_op jit(solution)/shard_map/dot_general | solution.py:501
  76.7 1.9 gather_fusion
  81.6 19.7 %reduce-scatter.2.cloned.1.call-done = bf16[128,1536]{1,0:T(8,128)(2,1)} async-done(((bf16[128,6144]{1,0:T(8,128)(2,1)}), bf16[128,1536]{1,0:T(8,128)(2,1)}) %reduce-scatter.2.cloned.1.call-update) | async-done | bytes 393232 | tf_op jit(solution)/shard_map/reduce_scatter | solution.py:504
  101.3 1.3 multiply_reduce_fusion.1
  102.6 5.9 %psum.7 = f32[128]{0:T(128)S(1)} all-reduce(f32[128]{0:T(128)S(1)} %multiply_reduce_fusion.1), channel_id=1, replica_groups=mesh['seq'=8,'head'=4] {'head'}, use_global_device_ids=true, to_apply=%region_5.6 | all-reduce | flops 128 | bytes 1024 | tf_op jit(solution)/shard_map/psum | solution.py:508
  108.5 2.4 convolution_convert_fusion.1
  110.9 66.1 %shard_map.118.act_ref = bf16[4,160,1152]{2,1,0:T(8,128)(2,1)} custom-call(f32[2]{0:T(128)} %pad_maximum_fusion.1.scale_ref, bf16[4,80,1536]{2,1,0:T(8,128)(2,1)} %bitcast.101, bf16[6144,1152]{1,0:T(8,128)(2,1)} %gate_ref.1, bf16[6144,1152]{1,0:T(8,128)(2,1)} %up_ref.1), custom_call_target="tpu_custom_call" | custom-call | tf_op jit(solution)/shard_map/pallas_call | solution.py:248
  177.0 66.1 %shard_map.119 = bf16[4,80,1536]{2,1,0:T(8,128)(2,1)} custom-call(f32[1]{0:T(128)S(6)} %mul.212.scale_ref, bf16[4,160,1152]{2,1,0:T(8,128)(2,1)} %shard_map.118.act_ref, bf16[1152,6144]{1,0:T(8,128)(2,1)} %down_ref.1), custom_call_target="tpu_custom_call" | custom-call | tf_op jit(solution)/shard_map/pallas_call | solution.py:425
  243.2 1.6 convolution_multiply_fusion.1
  244.8 2.4 fusion.2
  (61 shorter events, 5.8 us)
Async XLA Ops:
  6.5 2.8 %copy-start = (bf16[128,2048]{1,0:T(8,128)(2,1)S(1)}, bf16[128,2048]{1,0:T(8,128)(2,1)}, u32[]{:S(2)}) copy-start(bf16[128,2048]{1,0:T(8,128)(2,1)} %param.14) | copy-start | bytes 1572868
  10.5 22.4 %all-to-all-start = ((bf16[8,272,128]{2,1,0:T(8,128)(2,1)}), bf16[8,272,128]{2,1,0:T(8,128)(2,1)S(1)}, u32[]{:S(2)}, u32[]{:S(2)}) async-start(bf16[8,272,128]{2,1,0:T(8,128)(2,1)} %pad_maximum_fusion), calls=%async_computation | async-start | bytes 1114112 | tf_op jit(solution)/shard_map/all_to_all | solution.py:29
  38.2 18.3 %all-to-all-start.1 = ((bf16[8,256,128]{2,1,0:T(8,128)(2,1)}), bf16[8,256,128]{2,1,0:T(8,128)(2,1)S(1)}, u32[]{:S(2)}, u32[]{:S(2)}) async-start(bf16[8,256,128]{2,1,0:T(8,128)(2,1)} %fusion.34), calls=%async_computation.1 | async-start | bytes 1048576 | tf_op jit(solution)/shard_map/all_to_all | solution.py:36
  41.8 59.5 %reduce-scatter.2.cloned.1.call-start = ((), (), s32[]{:S(2)}) async-start(), calls=%async_computation.3 | async-start | bytes 1966080 | tf_op jit(solution)/shard_map/reduce_scatter | solution.py:504
  60.9 13.0 %copy-start.4 = (f32[14]{0:T(128)S(1)}, f32[14]{0:T(128)}, u32[]{:S(2)}) copy-start(f32[14]{0:T(128)} %param.23) | copy-start | bytes 172
  60.9 15.0 %copy-start.5 = (s32[128,2]{0,1:T(2,128)S(1)}, s32[128,2]{0,1:T(2,128)}, u32[]{:S(2)}) copy-start(s32[128,2]{0,1:T(2,128)} %param.18) | copy-start | bytes 3076
  76.7 4.8 %copy-start.6 = (f32[128,2]{0,1:T(2,128)S(1)}, f32[128,2]{0,1:T(2,128)}, u32[]{:S(2)}) copy-start(f32[128,2]{0,1:T(2,128)} %param.19) | copy-start | bytes 3076
  76.7 24.6 %copy-start.2 = (s32[128,1536]{1,0:T(8,128)S(1)}, s32[128,1536]{1,0:T(8,128)}, u32[]{:S(2)}) copy-start(s32[128,1536]{1,0:T(8,128)} %param.16) | copy-start | bytes 2359300
  177.0 67.8 %copy-start.3 = (bf16[128,1536]{1,0:T(8,128)(2,1)S(1)}, bf16[128,1536]{1,0:T(8,128)(2,1)}, u32[]{:S(2)}) copy-start(bf16[128,1536]{1,0:T(8,128)(2,1)} %reduce-scatter.2.cloned.1.call-done) | copy-start | bytes 1179652
  177.0 70.1 %copy-start.1 = (bf16[128,2048]{1,0:T(8,128)(2,1)S(1)}, bf16[128,2048]{1,0:T(8,128)(2,1)}, u32[]{:S(2)}) copy-start(bf16[128,2048]{1,0:T(8,128)(2,1)} %param.14) | copy-start | bytes 1572868
Sparse Core Ops, SparseCore 0:
  74.0 27.2 reduce-scatter.1
